TPU v7x, 512 devices: a whole 4x8x8 slice. The times are simulated.
512 devices in a mesh: row: 64 (over y, z), col: 8 (over x, core).
Axes of the slice: x: 4, y: 8, z: 8, core: 2. Of those that a mesh axis runs over, the one named last changes fastest.
Arguments:
- features: bfloat16 [65536, 512], P(('row', 'col')), may hold values from -6 to 6
- weight: bfloat16 [512, 512], replicated, may hold values from -0.25 to 0.25
- bias_vec: float32 [512], replicated, may hold values from -3 to 3
- tile_vals: bfloat16 [64, 8, 16, 128, 128], P('row', 'col'), may hold values from -0.1875 to 0.1875
- tile_coords: int32 [64, 8, 16, 2], P('row', 'col'), may hold values from 0 to 63, as said below
- tile_count: int32 [64, 8], P('row', 'col'), may hold values from 2 to 16, as said below
- cotangent: bfloat16 [65536, 512], P(('row', 'col')), may hold values from -6 to 6
Outputs:
- layer_out: bfloat16 [65536, 512], P(('row', 'col'))
- grad_weight: float32 [512, 512], replicated
- grad_bias: float32 [512], replicated
- grad_features: bfloat16 [65536, 512], P(('row', 'col'))
Inputs may be any that keep to these rules, and one draw needn't show every extreme that they name: tile_coords[r, c, s, 0] is below 8; tile_coords[r, c, s, 1] lies in the row bands r - 3 to r + 3 that exist. `tile_count`: some device has all 16 slots live.
All inputs are finite; a program needn't handle non-finite values.
Results may differ from a plain program's by a relative error of at most 0.019.
Values may be sent and summed in bfloat16 or wider, within the bound.
No kernel may reach another device: no remote copies, remote signals or barrier semaphores. Data moves between devices by JAX's collectives and lax.ppermute only.
A program may use at most 64 MiB of HBM per device.

v0:
```python
import jax
import jax.numpy as jnp
from jax import lax
from jax.sharding import PartitionSpec as P

REACH = 3


def passed_along(block, axis, distance):
    devices = range(lax.axis_size(axis))
    route = [(i - distance, i) for i in devices if i - distance in devices]
    return lax.ppermute(block, axis, route)


def gelu_tanh(values):
    return jax.nn.gelu(values, approximate=True)


def body(features, weight, bias_vec, tile_vals, tile_coords, tile_count, cotangent):
    col_count = lax.axis_size("col")
    own_row = lax.axis_index("row")
    tiles_here = tile_vals[0, 0]
    coords_here = tile_coords[0, 0]
    live_count = tile_count[0, 0]
    slot_count = tiles_here.shape[0]
    tile_size = features.shape[0]
    feat_width = features.shape[1]
    window = 2 * REACH + 1
    per_step = 8
    row_local = coords_here[:, 0]
    col_local = coords_here[:, 1]
    alive_mask = (jnp.arange(slot_count, dtype=jnp.int32) < live_count).astype(jnp.float32)
    window_index = col_local - own_row + REACH
    nearby = []
    for shift_by in range(-REACH, REACH + 1):
        if shift_by == 0:
            nearby.append(features)
        else:
            nearby.append(passed_along(features, "row", -shift_by))
    panels = jnp.stack(nearby)
    step_total = slot_count // per_step

    def slot_slices(group_idx):
        first_slot = group_idx * per_step
        tiles_now = lax.dynamic_slice_in_dim(tiles_here, first_slot, per_step, 0)
        alive_now = lax.dynamic_slice_in_dim(alive_mask, first_slot, per_step, 0)
        return (first_slot, tiles_now, alive_now)

    def forward_group(group_idx, totals):
        first_slot, tiles_now, alive_now = slot_slices(group_idx)
        col_pick = lax.dynamic_slice_in_dim(window_index, first_slot, per_step, 0)
        row_pick = lax.dynamic_slice_in_dim(row_local, first_slot, per_step, 0)
        picked = panels[col_pick]
        product = jnp.einsum("gij,gjf->gif", tiles_now, picked, preferred_element_type=jnp.float32)
        onehot = (row_pick[:, None] == jnp.arange(col_count, dtype=jnp.int32)[None, :]).astype(
            jnp.float32
        )
        onehot = onehot * alive_now[:, None]
        return totals + jnp.einsum("gb,gif->bif", onehot, product)

    partial_value = lax.fori_loop(
        0, step_total, forward_group, jnp.zeros((col_count, tile_size, feat_width), jnp.float32)
    )
    aggregate = lax.psum_scatter(
        partial_value.reshape(col_count * tile_size, feat_width),
        "col",
        scatter_dimension=0,
        tiled=True,
    )
    aggregate_b = aggregate.astype(jnp.bfloat16)
    pre_act = jnp.dot(aggregate_b, weight, preferred_element_type=jnp.float32) + bias_vec
    layer_out = gelu_tanh(pre_act).astype(jnp.bfloat16)
    unused_out, pullback = jax.vjp(gelu_tanh, pre_act)
    grad_pre = pullback(cotangent.astype(jnp.float32))[0].astype(jnp.bfloat16)
    weight_term = jnp.einsum("nf,ng->fg", aggregate_b, grad_pre, preferred_element_type=jnp.float32)
    bias_term = jnp.sum(grad_pre.astype(jnp.float32), axis=0)
    grad_weight, grad_bias = lax.psum((weight_term, bias_term), ("row", "col"))
    grad_mid = jnp.einsum("ng,fg->nf", grad_pre, weight, preferred_element_type=jnp.float32).astype(
        jnp.bfloat16
    )
    band_panels = lax.all_gather(grad_mid, "col", axis=0, tiled=True).reshape(
        col_count, tile_size, feat_width
    )

    def backward_group(group_idx, totals):
        first_slot, tiles_now, alive_now = slot_slices(group_idx)
        row_pick = lax.dynamic_slice_in_dim(row_local, first_slot, per_step, 0)
        win_pick = lax.dynamic_slice_in_dim(window_index, first_slot, per_step, 0)
        picked = band_panels[row_pick]
        product = jnp.einsum("gji,gjf->gif", tiles_now, picked, preferred_element_type=jnp.float32)
        onehot = (win_pick[:, None] == jnp.arange(window, dtype=jnp.int32)[None, :]).astype(
            jnp.float32
        )
        onehot = onehot * alive_now[:, None]
        return totals + jnp.einsum("gb,gif->bif", onehot, product)

    grad_acc = lax.fori_loop(
        0, step_total, backward_group, jnp.zeros((window, tile_size, feat_width), jnp.float32)
    )
    result_sum = grad_acc[REACH]
    for shift_by in range(-REACH, REACH + 1):
        if shift_by != 0:
            result_sum = result_sum + passed_along(grad_acc[shift_by + REACH], "row", shift_by)
    grad_features = result_sum.astype(jnp.bfloat16)
    return (layer_out, grad_weight, grad_bias, grad_features)


def solution(mesh):
    return jax.shard_map(
        body,
        mesh=mesh,
        in_specs=(
            P(("row", "col"), None),
            P(),
            P(),
            P("row", "col", None, None, None),
            P("row", "col", None, None),
            P("row", "col"),
            P(("row", "col"), None),
        ),
        out_specs=(P(("row", "col"), None), P(), P(), P(("row", "col"), None)),
        check_vma=False,
    )
```

profile of v0, /device:TPU:24, one launch (start us, length us, event | category | flops | bytes accessed | tf_op | source)
XLA Modules:
  0.0 473.3 jit_solution(12974934062237815644)
XLA Ops:
  7.2 8.0 %collective-permute-start = (bf16[128,512]{1,0:T(8,128)(2,1)}, bf16[128,512]{1,0:T(8,128)(2,1)S(1)}, u32[]{:S(2)}, u32[]{:S(2)}) collective-permute-start(bf16[128,512]{1,0:T(8,128)(2,1)} %param.11), channel_id=1, source_target_pairs={{0,24},{8,32},{16,40},{24,48},{32,56},{40,64},{48,72},{56,80},{64,... | collective-permute-start | bytes 393224 | tf_op jit(solution)/shard_map/ppermute | solution.py:12
  15.3 6.4 %collective-permute-start.1 = (bf16[128,512]{1,0:T(8,128)(2,1)}, bf16[128,512]{1,0:T(8,128)(2,1)S(1)}, u32[]{:S(2)}, u32[]{:S(2)}) collective-permute-start(bf16[128,512]{1,0:T(8,128)(2,1)} %param.11), channel_id=1, source_target_pairs={{0,16},{8,24},{16,32},{24,40},{32,48},{40,56},{48,64},{56,72},{64,... | collective-permute-start | bytes 393224 | tf_op jit(solution)/shard_map/ppermute | solution.py:12
  21.7 3.4 collective-permute-start.2
  25.1 4.6 collective-permute-start.3
  33.0 4.2 collective-permute-start.5
  38.2 2.6 collective-permute-done.4
  40.9 11.6 %collective-permute-done.5 = bf16[128,512]{1,0:T(8,128)(2,1)S(1)} collective-permute-done((bf16[128,512]{1,0:T(8,128)(2,1)}, bf16[128,512]{1,0:T(8,128)(2,1)S(1)}, u32[]{:S(2)}, u32[]{:S(2)}) %collective-permute-start.5) | collective-permute-done | bytes 131104 | tf_op jit(solution)/shard_map/ppermute | solution.py:12
  52.5 10.2 %while.28 = (s32[]{:T(128)}, f32[8,128,512]{2,0,1:T(8,128)}, s32[16]{0:T(128)S(1)}, bf16[16]{0:T(256)(128)(2,1)S(1)}, bf16[16,128,128]{2,1,0:T(8,128)(2,1)}, /*i...) while((s32[]{:T(128)}, f32[8,128,512]{2,0,1:T(8,128)}, ...), condition=%wide.region_1.0_spmd.clone, body=%wide.region_0.0_spmd.clone.sunk | while | flops 143656096 | bytes 9703877 | solution.py:61
  59.1 3.7 select_add_fusion.4
  62.7 4.1 copy.18
  67.0 33.2 %reduce-scatter.2.cloned.1.call-done = f32[128,512]{1,0:T(8,128)} async-done(((f32[1024,512]{1,0:T(8,128)}), f32[128,512]{1,0:T(8,128)}) %reduce-scatter.2.cloned.1.call-update) | async-done | bytes 262160 | tf_op jit(solution)/shard_map/reduce_scatter | solution.py:64
  103.2 27.5 %all-gather.2.cloned.1.call-done = bf16[1024,512]{1,0:T(8,128)(2,1)} async-done(((bf16[128,512]{1,0:T(8,128)(2,1)}), bf16[1024,512]{1,0:T(8,128)(2,1)}) %all-gather.2.cloned.1.call-update) | async-done | bytes 1048592 | tf_op jit(solution)/shard_map/all_gather | solution.py:81
  130.8 11.0 %while.29 = (s32[]{:T(128)}, f32[7,128,512]{2,0,1:T(8,128)}, s32[16]{0:T(128)S(1)}, bf16[16]{0:T(256)(128)(2,1)S(1)}, bf16[16,128,128]{2,1,0:T(8,128)(2,1)S(1)},...) while((s32[]{:T(128)}, f32[7,128,512]{2,0,1:T(8,128)}, ...), condition=%wide.region_7.0_spmd.clone, body=%wide.region_6.0_spmd.clone.sunk | while | flops 142476432 | bytes 9179589 | solution.py:97
  138.1 3.7 select_add_fusion.5
  141.8 2.7 copy.19
  145.4 4.6 collective-permute-start.10
  150.1 6.0 %collective-permute-start.11 = (f32[128,512]{1,0:T(8,128)}, f32[128,512]{1,0:T(8,128)S(1)}, u32[]{:S(2)}, u32[]{:S(2)}) collective-permute-start(f32[128,512]{1,0:T(8,128)} %get-tuple-element.333), channel_id=1, source_target_pairs={{0,24},{8,32},{16,40},{24,48},{32,56},{40,64},{48,72},{56,80},{64,... | collective-permute-start | bytes 786440 | tf_op jit(solution)/shard_map/ppermute | solution.py:12
  156.1 3.7 collective-permute-start.6
  159.8 3.3 collective-permute-start.7
  163.2 3.7 collective-permute-start.8
  168.5 3.8 collective-permute-start.9
  173.7 123.1 %psum.15 = f32[512]{0:T(512)} all-reduce(f32[512]{0:T(512)S(1)} %get-tuple-element.330), channel_id=1, replica_groups=mesh['row'=64,'col'=8] {'row','col'}, use_global_device_ids=true, to_apply=%region_5.0 | all-reduce | flops 512 | bytes 4096 | tf_op jit(solution)/shard_map/psum | solution.py:77
  298.9 165.6 %all-reduce.2.cloned.1.call-done = f32[512,512]{1,0:T(8,128)} async-done(((f32[512,512]{1,0:T(8,128)}), f32[512,512]{1,0:T(8,128)}) %all-reduce.2.cloned.1.call-update) | async-done | bytes 1048592 | tf_op jit(solution)/shard_map/psum | solution.py:77
  464.5 2.3 copy.60
  (69 shorter events, 26.5 us)
Async XLA Ops:
  7.2 93.0 %copy-start = (bf16[512,512]{1,0:T(8,128)(2,1)S(1)}, bf16[512,512]{1,0:T(8,128)(2,1)}, u32[]{:S(2)}) copy-start(bf16[512,512]{1,0:T(8,128)(2,1)} %param.12) | copy-start | bytes 1572868
  7.2 93.0 %reduce-scatter.2.cloned.1.call-start = ((), (), s32[]{:S(2)}) async-start(), calls=%async_computation.1 | async-start | bytes 2359296 | tf_op jit(solution)/shard_map/reduce_scatter | solution.py:64
  7.2 25.8 %collective-permute-start = (bf16[128,512]{1,0:T(8,128)(2,1)}, bf16[128,512]{1,0:T(8,128)(2,1)S(1)}, u32[]{:S(2)}, u32[]{:S(2)}) collective-permute-start(bf16[128,512]{1,0:T(8,128)(2,1)} %param.11), channel_id=1, source_target_pairs={{0,24},{8,32},{16,40},{24,48},{32,56},{40,64},{48,72},{56,80},{64,... | collective-permute-start | bytes 393224 | tf_op jit(solution)/shard_map/ppermute | solution.py:12
  15.3 22.0 %collective-permute-start.1 = (bf16[128,512]{1,0:T(8,128)(2,1)}, bf16[128,512]{1,0:T(8,128)(2,1)S(1)}, u32[]{:S(2)}, u32[]{:S(2)}) collective-permute-start(bf16[128,512]{1,0:T(8,128)(2,1)} %param.11), channel_id=1, source_target_pairs={{0,16},{8,24},{16,32},{24,40},{32,48},{40,56},{48,64},{56,72},{64,... | collective-permute-start | bytes 393224 | tf_op jit(solution)/shard_map/ppermute | solution.py:12
  21.7 15.6 %collective-permute-start.2 = (bf16[128,512]{1,0:T(8,128)(2,1)}, bf16[128,512]{1,0:T(8,128)(2,1)S(1)}, u32[]{:S(2)}, u32[]{:S(2)}) collective-permute-start(bf16[128,512]{1,0:T(8,128)(2,1)} %param.11), channel_id=1, source_target_pairs={{0,8},{8,16},{16,24},{24,32},{32,40},{40,48},{48,56},{56,64},{64,7... | collective-permute-start | bytes 393224 | tf_op jit(solution)/shard_map/ppermute | solution.py:12
  25.1 13.1 %collective-permute-start.3 = (bf16[128,512]{1,0:T(8,128)(2,1)}, bf16[128,512]{1,0:T(8,128)(2,1)S(1)}, u32[]{:S(2)}, u32[]{:S(2)}) collective-permute-start(bf16[128,512]{1,0:T(8,128)(2,1)} %param.11), channel_id=1, source_target_pairs={{8,0},{16,8},{24,16},{32,24},{40,32},{48,40},{56,48},{64,56},{72,6... | collective-permute-start | bytes 393224 | tf_op jit(solution)/shard_map/ppermute | solution.py:12
  29.6 11.2 %collective-permute-start.4 = (bf16[128,512]{1,0:T(8,128)(2,1)}, bf16[128,512]{1,0:T(8,128)(2,1)S(1)}, u32[]{:S(2)}, u32[]{:S(2)}) collective-permute-start(bf16[128,512]{1,0:T(8,128)(2,1)} %param.11), channel_id=1, source_target_pairs={{16,0},{24,8},{32,16},{40,24},{48,32},{56,40},{64,48},{72,56},{80,... | collective-permute-start | bytes 393224 | tf_op jit(solution)/shard_map/ppermute | solution.py:12
  33.0 19.5 %collective-permute-start.5 = (bf16[128,512]{1,0:T(8,128)(2,1)}, bf16[128,512]{1,0:T(8,128)(2,1)S(1)}, u32[]{:S(2)}, u32[]{:S(2)}) collective-permute-start(bf16[128,512]{1,0:T(8,128)(2,1)} %param.11), channel_id=1, source_target_pairs={{24,0},{32,8},{40,16},{48,24},{56,32},{64,40},{72,48},{80,56},{88,... | collective-permute-start | bytes 393224 | tf_op jit(solution)/shard_map/ppermute | solution.py:12
  66.9 33.3 %copy-start.3 = (bf16[128,512]{1,0:T(8,128)(2,1)S(1)}, bf16[128,512]{1,0:T(8,128)(2,1)}, u32[]{:S(2)}) copy-start(bf16[128,512]{1,0:T(8,128)(2,1)} %param.17) | copy-start | bytes 393220
  66.9 33.3 %copy-start.4 = (f32[512]{0:T(512)S(1)}, f32[512]{0:T(512)}, u32[]{:S(2)}) copy-start(f32[512]{0:T(512)} %param.13) | copy-start | bytes 6148
  66.9 63.9 %copy-start.1 = (bf16[16,128,128]{2,1,0:T(8,128)(2,1)S(1)}, bf16[16,128,128]{2,1,0:T(8,128)(2,1)}, u32[]{:S(2)}) copy-start(bf16[16,128,128]{2,1,0:T(8,128)(2,1)} %get-tuple-element.501) | copy-start | bytes 1572868
  66.9 63.9 %all-gather.2.cloned.1.call-start = ((), (), s32[]{:S(2)}) async-start(), calls=%async_computation.3 | async-start | bytes 1179648 | tf_op jit(solution)/shard_map/all_gather | solution.py:81
  103.2 361.3 %all-reduce.2.cloned.1.call-start = ((), (), s32[]{:S(2)}) async-start(), calls=%async_computation.2 | async-start | bytes 2097152 | tf_op jit(solution)/shard_map/psum | solution.py:77
  144.5 27.9 %copy-start.2 = (f32[128,512]{1,0:T(8,128)S(1)}, f32[128,512]{1,0:T(8,128)}, u32[]{:S(2)}) copy-start(f32[128,512]{1,0:T(8,128)} %reduce-scatter.2.cloned.1.call-done) | copy-start | bytes 786436
  145.4 23.1 %collective-permute-start.10 = (f32[128,512]{1,0:T(8,128)S(1)}, f32[128,512]{1,0:T(8,128)S(1)}, u32[]{:S(2)}, u32[]{:S(2)}) collective-permute-start(f32[128,512]{1,0:T(8,128)S(1)} %get-tuple-element.334), channel_id=1, source_target_pairs={{0,16},{8,24},{16,32},{24,40},{32,48},{40,56},{48,64},{56,72},{64,... | collective-permute-start | bytes 786440 | tf_op jit(solution)/shard_map/ppermute | solution.py:12
  150.1 146.8 %collective-permute-start.11 = (f32[128,512]{1,0:T(8,128)}, f32[128,512]{1,0:T(8,128)S(1)}, u32[]{:S(2)}, u32[]{:S(2)}) collective-permute-start(f32[128,512]{1,0:T(8,128)} %get-tuple-element.333), channel_id=1, source_target_pairs={{0,24},{8,32},{16,40},{24,48},{32,56},{40,64},{48,72},{56,80},{64,... | collective-permute-start | bytes 786440 | tf_op jit(solution)/shard_map/ppermute | solution.py:12
  156.1 140.7 %collective-permute-start.6 = (f32[128,512]{1,0:T(8,128)}, f32[128,512]{1,0:T(8,128)}, u32[]{:S(2)}, u32[]{:S(2)}) collective-permute-start(f32[128,512]{1,0:T(8,128)} %get-tuple-element.332), channel_id=1, source_target_pairs={{24,0},{32,8},{40,16},{48,24},{56,32},{64,40},{72,48},{80,56},{88,... | collective-permute-start | bytes 786440 | tf_op jit(solution)/shard_map/ppermute | solution.py:12
  159.8 137.0 %collective-permute-start.7 = (f32[128,512]{1,0:T(8,128)}, f32[128,512]{1,0:T(8,128)}, u32[]{:S(2)}, u32[]{:S(2)}) collective-permute-start(f32[128,512]{1,0:T(8,128)} %get-tuple-element.337), channel_id=1, source_target_pairs={{16,0},{24,8},{32,16},{40,24},{48,32},{56,40},{64,48},{72,56},{80,... | collective-permute-start | bytes 786440 | tf_op jit(solution)/shard_map/ppermute | solution.py:12
  163.2 133.7 %collective-permute-start.8 = (f32[128,512]{1,0:T(8,128)S(1)}, f32[128,512]{1,0:T(8,128)}, u32[]{:S(2)}, u32[]{:S(2)}) collective-permute-start(f32[128,512]{1,0:T(8,128)S(1)} %get-tuple-element.336), channel_id=1, source_target_pairs={{8,0},{16,8},{24,16},{32,24},{40,32},{48,40},{56,48},{64,56},{72,6... | collective-permute-start | bytes 786440 | tf_op jit(solution)/shard_map/ppermute | solution.py:12
  168.5 128.3 %collective-permute-start.9 = (f32[128,512]{1,0:T(8,128)S(1)}, f32[128,512]{1,0:T(8,128)}, u32[]{:S(2)}, u32[]{:S(2)}) collective-permute-start(f32[128,512]{1,0:T(8,128)S(1)} %get-tuple-element.335), channel_id=1, source_target_pairs={{0,8},{8,16},{16,24},{24,32},{32,40},{40,48},{48,56},{56,64},{64,7... | collective-permute-start | bytes 786440 | tf_op jit(solution)/shard_map/ppermute | solution.py:12
Sparse Core Ops, SparseCore 0:
  67.0 33.0 reduce-scatter.1
  103.3 27.4 all-gather.1
  173.8 290.6 all-reduce.1
where the time goes:
time: 474 us; the launch traced here: 473 us
  waiting for transfers between devices  242 us (51%)
  blocking collectives  123 us (26%)
  starting transfers between devices  53.9 us (11%)
  matrix products  19.6 us (4%)
  local copies, waits for them, and re-layouts  16.5 us (3%)
  between operations  14.6 us (3%)
    psum x1, waiting for transfers between devices, body(): grad_weight, grad_bias = lax.psum((weight_term, bias_term), ('row', 'col'))  166 us
    psum x1, blocking collectives, body(): grad_weight, grad_bias = lax.psum((weight_term, bias_term), ('row', 'col'))  123 us
    ppermute x12, starting transfers between devices, passed_along(): return lax.ppermute(block, axis, route)  53.8 us
    reduce_scatter x1, waiting for transfers between devices, body(): lax.psum_scatter(partial_value.reshape(col_count * tile_size, feat_width)...  33.2 us
    all_gather x1, waiting for transfers between devices, body(): lax.all_gather(grad_mid, 'col', axis=0, tiled=True)  27.5 us
    ppermute x12, waiting for transfers between devices, passed_along(): return lax.ppermute(block, axis, route)  15.9 us
  transfers between devices with their start and end apart: 15, of which 6 were waited for; matrix products, arithmetic and copies ran while one was open for 1% of the time, Pallas kernels for 0%

commit v1 on v0

--- a/solution.py
+++ b/solution.py
@@ -74,7 +74,8 @@
     grad_pre = pullback(cotangent.astype(jnp.float32))[0].astype(jnp.bfloat16)
     weight_term = jnp.einsum("nf,ng->fg", aggregate_b, grad_pre, preferred_element_type=jnp.float32)
     bias_term = jnp.sum(grad_pre.astype(jnp.float32), axis=0)
-    grad_weight, grad_bias = lax.psum((weight_term, bias_term), ("row", "col"))
+    streams_finish = lambda base_x: lax.psum(lax.psum(base_x, axis_name="row"), axis_name="col")
+    grad_weight, grad_bias = streams_finish((weight_term, bias_term))
     grad_mid = jnp.einsum("ng,fg->nf", grad_pre, weight, preferred_element_type=jnp.float32).astype(
         jnp.bfloat16
     )

time: 474 us -> 501 us (1.057)
  the two profiles are of different devices: /device:TPU:24 before, /device:TPU:1 now
where the time goes in v1:
time: 501 us; the launch traced here: 500 us
  waiting for transfers between devices  239 us (48%)
  blocking collectives  158 us (32%)
  starting transfers between devices  48.8 us (10%)
  matrix products  19.7 us (4%)
  local copies, waits for them, and re-layouts  16.6 us (3%)
  between operations  14.7 us (3%)
    psum x1, waiting for transfers between devices, body(): lax.psum(base_x, axis_name='row')  157 us
    psum x1, blocking collectives, body(): lax.psum(base_x, axis_name='row')  113 us
    ppermute x12, starting transfers between devices, passed_along(): return lax.ppermute(block, axis, route)  48.7 us
    psum x1, blocking collectives, body(): lax.psum(lax.psum(base_x, axis_name='row'), axis_name='col')  44.8 us
    reduce_scatter x1, waiting for transfers between devices, body(): lax.psum_scatter(partial_value.reshape(col_count * tile_size, feat_width)...  34.3 us
    all_gather x1, waiting for transfers between devices, body(): lax.all_gather(grad_mid, 'col', axis=0, tiled=True)  28.7 us
    ppermute x12, waiting for transfers between devices, passed_along(): return lax.ppermute(block, axis, route)  19.3 us
  transfers between devices with their start and end apart: 16, of which 5 were waited for; matrix products, arithmetic and copies ran while one was open for 4% of the time, Pallas kernels for 0%

profile of v1, /device:TPU:1, one launch (start us, length us, event | category | flops | bytes accessed | tf_op | source)
XLA Modules:
  0.0 500.0 jit_solution(13246829573797859506)
XLA Ops:
  7.2 8.6 %collective-permute-start = (bf16[128,512]{1,0:T(8,128)(2,1)}, bf16[128,512]{1,0:T(8,128)(2,1)S(1)}, u32[]{:S(2)}, u32[]{:S(2)}) collective-permute-start(bf16[128,512]{1,0:T(8,128)(2,1)} %param.11), channel_id=1, source_target_pairs={{0,24},{8,32},{16,40},{24,48},{32,56},{40,64},{48,72},{56,80},{64,... | collective-permute-start | bytes 393224 | tf_op jit(solution)/shard_map/ppermute | solution.py:12
  15.8 6.1 %collective-permute-start.1 = (bf16[128,512]{1,0:T(8,128)(2,1)}, bf16[128,512]{1,0:T(8,128)(2,1)S(1)}, u32[]{:S(2)}, u32[]{:S(2)}) collective-permute-start(bf16[128,512]{1,0:T(8,128)(2,1)} %param.11), channel_id=1, source_target_pairs={{0,16},{8,24},{16,32},{24,40},{32,48},{40,56},{48,64},{56,72},{64,... | collective-permute-start | bytes 393224 | tf_op jit(solution)/shard_map/ppermute | solution.py:12
  22.0 3.1 collective-permute-start.2
  31.4 6.2 %collective-permute-done.4 = bf16[128,512]{1,0:T(8,128)(2,1)S(1)} collective-permute-done((bf16[128,512]{1,0:T(8,128)(2,1)}, bf16[128,512]{1,0:T(8,128)(2,1)S(1)}, u32[]{:S(2)}, u32[]{:S(2)}) %collective-permute-start.4) | collective-permute-done | bytes 131104 | tf_op jit(solution)/shard_map/ppermute | solution.py:12
  37.6 13.1 %collective-permute-done.5 = bf16[128,512]{1,0:T(8,128)(2,1)S(1)} collective-permute-done((bf16[128,512]{1,0:T(8,128)(2,1)}, bf16[128,512]{1,0:T(8,128)(2,1)S(1)}, u32[]{:S(2)}, u32[]{:S(2)}) %collective-permute-start.5) | collective-permute-done | bytes 131104 | tf_op jit(solution)/shard_map/ppermute | solution.py:12
  50.7 10.3 %while.28 = (s32[]{:T(128)}, f32[8,128,512]{2,0,1:T(8,128)}, s32[16]{0:T(128)S(1)}, bf16[16]{0:T(256)(128)(2,1)S(1)}, bf16[16,128,128]{2,1,0:T(8,128)(2,1)}, /*i...) while((s32[]{:T(128)}, f32[8,128,512]{2,0,1:T(8,128)}, ...), condition=%wide.region_1.0_spmd.clone, body=%wide.region_0.0_spmd.clone.sunk | while | flops 143656096 | bytes 9703877 | solution.py:61
  53.0 2.1 select_add_fusion.4
  57.3 3.7 select_add_fusion.4
  61.0 4.1 copy.18
  65.2 34.3 %reduce-scatter.2.cloned.1.call-done = f32[128,512]{1,0:T(8,128)} async-done(((f32[1024,512]{1,0:T(8,128)}), f32[128,512]{1,0:T(8,128)}) %reduce-scatter.2.cloned.1.call-update) | async-done | bytes 262160 | tf_op jit(solution)/shard_map/reduce_scatter | solution.py:64
  99.5 2.1 convert_reduce_fusion
  104.0 28.7 %all-gather.2.cloned.1.call-done = bf16[1024,512]{1,0:T(8,128)(2,1)} async-done(((bf16[128,512]{1,0:T(8,128)(2,1)}), bf16[1024,512]{1,0:T(8,128)(2,1)}) %all-gather.2.cloned.1.call-update) | async-done | bytes 1048592 | tf_op jit(solution)/shard_map/all_gather | solution.py:82
  132.7 11.0 %while.29 = (s32[]{:T(128)}, f32[7,128,512]{2,0,1:T(8,128)}, s32[16]{0:T(128)S(1)}, bf16[16]{0:T(256)(128)(2,1)S(1)}, bf16[16,128,128]{2,1,0:T(8,128)(2,1)S(1)},...) while((s32[]{:T(128)}, f32[7,128,512]{2,0,1:T(8,128)}, ...), condition=%wide.region_9.0_spmd.clone, body=%wide.region_8.0_spmd.clone.sunk | while | flops 142476432 | bytes 9179589 | solution.py:98
  135.2 2.1 select_add_fusion.5
  140.0 3.7 select_add_fusion.5
  143.7 2.7 copy.19
  147.3 4.2 collective-permute-start.10
  151.5 5.7 %collective-permute-start.11 = (f32[128,512]{1,0:T(8,128)}, f32[128,512]{1,0:T(8,128)S(1)}, u32[]{:S(2)}, u32[]{:S(2)}) collective-permute-start(f32[128,512]{1,0:T(8,128)} %get-tuple-element.333), channel_id=1, source_target_pairs={{0,24},{8,32},{16,40},{24,48},{32,56},{40,64},{48,72},{56,80},{64,... | collective-permute-start | bytes 786440 | tf_op jit(solution)/shard_map/ppermute | solution.py:12
  161.2 13.2 %collective-permute-start.9 = (f32[128,512]{1,0:T(8,128)S(1)}, f32[128,512]{1,0:T(8,128)}, u32[]{:S(2)}, u32[]{:S(2)}) collective-permute-start(f32[128,512]{1,0:T(8,128)S(1)} %get-tuple-element.335), channel_id=1, source_target_pairs={{0,8},{8,16},{16,24},{24,32},{32,40},{40,48},{48,56},{56,64},{64,7... | collective-permute-start | bytes 786440 | tf_op jit(solution)/shard_map/ppermute | solution.py:12
  174.3 156.8 %all-reduce.3.cloned.1.call-done = f32[512,512]{1,0:T(8,128)} async-done(((f32[512,512]{1,0:T(8,128)}), f32[512,512]{1,0:T(8,128)}) %all-reduce.3.cloned.1.call-update) | async-done | bytes 1048592 | tf_op jit(solution)/shard_map/psum | solution.py:77
  331.1 113.3 %psum.30 = f32[512]{0:T(512)S(1)} all-reduce(f32[512]{0:T(512)S(1)} %get-tuple-element.330), channel_id=1, replica_groups=mesh['row'=64,'col'=8] {'row'}, use_global_device_ids=true, to_apply=%region_6.0 | all-reduce | flops 512 | bytes 4096 | tf_op jit(solution)/shard_map/psum | solution.py:77
  444.5 44.8 %psum.31 = f32[512]{0:T(512)} all-reduce(f32[512]{0:T(512)S(1)} %psum.30), channel_id=1, replica_groups=mesh['row'=64,'col'=8] {'col'}, use_global_device_ids=true, to_apply=%region_7.0 | all-reduce | flops 512 | bytes 4096 | tf_op jit(solution)/shard_map/psum | solution.py:77
  489.3 2.0 fusion.42
  491.2 2.3 copy.61
  (73 shorter events, 22.6 us)
Async XLA Ops:
  7.2 92.3 %copy-start = (bf16[512,512]{1,0:T(8,128)(2,1)S(1)}, bf16[512,512]{1,0:T(8,128)(2,1)}, u32[]{:S(2)}) copy-start(bf16[512,512]{1,0:T(8,128)(2,1)} %param.12) | copy-start | bytes 1572868
  7.2 92.3 %reduce-scatter.2.cloned.1.call-start = ((), (), s32[]{:S(2)}) async-start(), calls=%async_computation.1 | async-start | bytes 2359296 | tf_op jit(solution)/shard_map/reduce_scatter | solution.py:64
  7.2 21.9 %collective-permute-start = (bf16[128,512]{1,0:T(8,128)(2,1)}, bf16[128,512]{1,0:T(8,128)(2,1)S(1)}, u32[]{:S(2)}, u32[]{:S(2)}) collective-permute-start(bf16[128,512]{1,0:T(8,128)(2,1)} %param.11), channel_id=1, source_target_pairs={{0,24},{8,32},{16,40},{24,48},{32,56},{40,64},{48,72},{56,80},{64,... | collective-permute-start | bytes 393224 | tf_op jit(solution)/shard_map/ppermute | solution.py:12
  15.8 14.6 %collective-permute-start.1 = (bf16[128,512]{1,0:T(8,128)(2,1)}, bf16[128,512]{1,0:T(8,128)(2,1)S(1)}, u32[]{:S(2)}, u32[]{:S(2)}) collective-permute-start(bf16[128,512]{1,0:T(8,128)(2,1)} %param.11), channel_id=1, source_target_pairs={{0,16},{8,24},{16,32},{24,40},{32,48},{40,56},{48,64},{56,72},{64,... | collective-permute-start | bytes 393224 | tf_op jit(solution)/shard_map/ppermute | solution.py:12
  22.0 8.5 %collective-permute-start.2 = (bf16[128,512]{1,0:T(8,128)(2,1)}, bf16[128,512]{1,0:T(8,128)(2,1)S(1)}, u32[]{:S(2)}, u32[]{:S(2)}) collective-permute-start(bf16[128,512]{1,0:T(8,128)(2,1)} %param.11), channel_id=1, source_target_pairs={{0,8},{8,16},{16,24},{24,32},{32,40},{40,48},{48,56},{56,64},{64,7... | collective-permute-start | bytes 393224 | tf_op jit(solution)/shard_map/ppermute | solution.py:12
  25.1 6.3 %collective-permute-start.3 = (bf16[128,512]{1,0:T(8,128)(2,1)}, bf16[128,512]{1,0:T(8,128)(2,1)S(1)}, u32[]{:S(2)}, u32[]{:S(2)}) collective-permute-start(bf16[128,512]{1,0:T(8,128)(2,1)} %param.11), channel_id=1, source_target_pairs={{8,0},{16,8},{24,16},{32,24},{40,32},{48,40},{56,48},{64,56},{72,6... | collective-permute-start | bytes 393224 | tf_op jit(solution)/shard_map/ppermute | solution.py:12
  26.4 11.2 %collective-permute-start.4 = (bf16[128,512]{1,0:T(8,128)(2,1)}, bf16[128,512]{1,0:T(8,128)(2,1)S(1)}, u32[]{:S(2)}, u32[]{:S(2)}) collective-permute-start(bf16[128,512]{1,0:T(8,128)(2,1)} %param.11), channel_id=1, source_target_pairs={{16,0},{24,8},{32,16},{40,24},{48,32},{56,40},{64,48},{72,56},{80,... | collective-permute-start | bytes 393224 | tf_op jit(solution)/shard_map/ppermute | solution.py:12
  29.1 21.6 %collective-permute-start.5 = (bf16[128,512]{1,0:T(8,128)(2,1)}, bf16[128,512]{1,0:T(8,128)(2,1)S(1)}, u32[]{:S(2)}, u32[]{:S(2)}) collective-permute-start(bf16[128,512]{1,0:T(8,128)(2,1)} %param.11), channel_id=1, source_target_pairs={{24,0},{32,8},{40,16},{48,24},{56,32},{64,40},{72,48},{80,56},{88,... | collective-permute-start | bytes 393224 | tf_op jit(solution)/shard_map/ppermute | solution.py:12
  65.1 34.4 %copy-start.3 = (bf16[128,512]{1,0:T(8,128)(2,1)S(1)}, bf16[128,512]{1,0:T(8,128)(2,1)}, u32[]{:S(2)}) copy-start(bf16[128,512]{1,0:T(8,128)(2,1)} %param.17) | copy-start | bytes 393220
  65.1 34.4 %copy-start.4 = (f32[512]{0:T(512)S(1)}, f32[512]{0:T(512)}, u32[]{:S(2)}) copy-start(f32[512]{0:T(512)} %param.13) | copy-start | bytes 6148
  65.1 67.5 %all-gather.2.cloned.1.call-start = ((), (), s32[]{:S(2)}) async-start(), calls=%async_computation.4 | async-start | bytes 1179648 | tf_op jit(solution)/shard_map/all_gather | solution.py:82
  99.5 3.2 copy-start.2
  101.6 31.1 %copy-start.1 = (bf16[16,128,128]{2,1,0:T(8,128)(2,1)S(1)}, bf16[16,128,128]{2,1,0:T(8,128)(2,1)}, u32[]{:S(2)}) copy-start(bf16[16,128,128]{2,1,0:T(8,128)(2,1)} %get-tuple-element.502) | copy-start | bytes 1572868
  102.6 228.5 %all-reduce.3.cloned.1.call-start = ((), (), s32[]{:S(2)}) async-start(), calls=%async_computation.2 | async-start | bytes 2097152 | tf_op jit(solution)/shard_map/psum | solution.py:77
  104.0 387.3 %all-reduce.5.cloned.1.call-start = ((), (), s32[]{:S(2)}) async-start(), calls=%async_computation.3 | async-start | bytes 2097152 | tf_op jit(solution)/shard_map/psum | solution.py:77
  147.3 13.9 %collective-permute-start.10 = (f32[128,512]{1,0:T(8,128)S(1)}, f32[128,512]{1,0:T(8,128)S(1)}, u32[]{:S(2)}, u32[]{:S(2)}) collective-permute-start(f32[128,512]{1,0:T(8,128)S(1)} %get-tuple-element.334), channel_id=1, source_target_pairs={{0,16},{8,24},{16,32},{24,40},{32,48},{40,56},{48,64},{56,72},{64,... | collective-permute-start | bytes 786440 | tf_op jit(solution)/shard_map/ppermute | solution.py:12
  151.5 337.7 %collective-permute-start.11 = (f32[128,512]{1,0:T(8,128)}, f32[128,512]{1,0:T(8,128)S(1)}, u32[]{:S(2)}, u32[]{:S(2)}) collective-permute-start(f32[128,512]{1,0:T(8,128)} %get-tuple-element.333), channel_id=1, source_target_pairs={{0,24},{8,32},{16,40},{24,48},{32,56},{40,64},{48,72},{56,80},{64,... | collective-permute-start | bytes 786440 | tf_op jit(solution)/shard_map/ppermute | solution.py:12
  157.3 332.0 %collective-permute-start.6 = (f32[128,512]{1,0:T(8,128)}, f32[128,512]{1,0:T(8,128)}, u32[]{:S(2)}, u32[]{:S(2)}) collective-permute-start(f32[128,512]{1,0:T(8,128)} %get-tuple-element.332), channel_id=1, source_target_pairs={{24,0},{32,8},{40,16},{48,24},{56,32},{64,40},{72,48},{80,56},{88,... | collective-permute-start | bytes 786440 | tf_op jit(solution)/shard_map/ppermute | solution.py:12
  158.6 330.7 %collective-permute-start.7 = (f32[128,512]{1,0:T(8,128)}, f32[128,512]{1,0:T(8,128)}, u32[]{:S(2)}, u32[]{:S(2)}) collective-permute-start(f32[128,512]{1,0:T(8,128)} %get-tuple-element.337), channel_id=1, source_target_pairs={{16,0},{24,8},{32,16},{40,24},{48,32},{56,40},{64,48},{72,56},{80,... | collective-permute-start | bytes 786440 | tf_op jit(solution)/shard_map/ppermute | solution.py:12
  159.9 329.4 %collective-permute-start.8 = (f32[128,512]{1,0:T(8,128)S(1)}, f32[128,512]{1,0:T(8,128)}, u32[]{:S(2)}, u32[]{:S(2)}) collective-permute-start(f32[128,512]{1,0:T(8,128)S(1)} %get-tuple-element.336), channel_id=1, source_target_pairs={{8,0},{16,8},{24,16},{32,24},{40,32},{48,40},{56,48},{64,56},{72,6... | collective-permute-start | bytes 786440 | tf_op jit(solution)/shard_map/ppermute | solution.py:12
  161.2 328.1 %collective-permute-start.9 = (f32[128,512]{1,0:T(8,128)S(1)}, f32[128,512]{1,0:T(8,128)}, u32[]{:S(2)}, u32[]{:S(2)}) collective-permute-start(f32[128,512]{1,0:T(8,128)S(1)} %get-tuple-element.335), channel_id=1, source_target_pairs={{0,8},{8,16},{16,24},{24,32},{32,40},{40,48},{48,56},{56,64},{64,7... | collective-permute-start | bytes 786440 | tf_op jit(solution)/shard_map/ppermute | solution.py:12
Sparse Core Ops, SparseCore 0:
  65.3 34.1 reduce-scatter.1
  102.7 29.9 all-gather.1
  136.4 194.6 all-reduce.2
  333.4 71.9 all-reduce.4
